TPU v7x, 256 devices: a whole 4x4x8 slice. The times are simulated.
256 devices in a mesh: rows: 8 (over y, core), cols: 32 (over x, z).
Axes of the slice: x: 4, y: 4, z: 8, core: 2. Of those that a mesh axis runs over, the one named last changes fastest.
Arguments:
- out_grad: bfloat16 [2048, 8192], P('rows', 'cols'), may hold values from -6 to 6
- gate_act: bfloat16 [2048, 28672], P('cols', 'rows'), may hold values from -8 to 8
- up_act: bfloat16 [2048, 28672], P('cols', 'rows'), may hold values from -6 to 6
- down_weight: bfloat16 [28672, 8192], P('rows', 'cols'), may hold values from -0.03125 to 0.03125
Outputs:
- weight_grad: float32 [28672, 8192], P('rows', 'cols')
- gate_grad: bfloat16 [2048, 28672], P('cols', 'rows')
- up_grad: bfloat16 [2048, 28672], P('cols', 'rows')
All inputs are finite; a program needn't handle non-finite values.
Results may differ from a plain program's by a relative error of at most 0.034.
Values may be sent and summed in bfloat16 or wider, within the bound.
A program may use at most 128 MiB of HBM per device.

v0:
```python
import jax
import jax.numpy as jnp
from jax import lax
from jax.sharding import PartitionSpec as P


def hidden_from(gate_part, up_part):
    gate_wide = gate_part.astype(jnp.float32)
    sigmoid_gate = jax.nn.sigmoid(gate_wide)
    swish = gate_wide * sigmoid_gate
    return (sigmoid_gate, swish, (swish * up_part.astype(jnp.float32)).astype(jnp.bfloat16))


def shards(out_grad, gate_act, up_act, down_weight):
    grads_all = lax.all_gather(out_grad, "rows", axis=0, tiled=True)
    hidden_grad = lax.psum_scatter(
        lax.dot_general(
            grads_all, down_weight, (((1,), (1,)), ((), ())), preferred_element_type=jnp.float32
        ).astype(jnp.bfloat16),
        "cols",
        scatter_dimension=0,
        tiled=True,
    ).astype(jnp.float32)
    sigmoid_gate, swish, hidden = hidden_from(gate_act, up_act)
    gate_wide = gate_act.astype(jnp.float32)
    up_wide = up_act.astype(jnp.float32)
    gate_grad = (
        hidden_grad * up_wide * sigmoid_gate * (1.0 + gate_wide * (1.0 - sigmoid_gate))
    ).astype(jnp.bfloat16)
    up_grad = (hidden_grad * swish).astype(jnp.bfloat16)
    unused_sig, unused_swish, hidden_piece = hidden_from(
        lax.all_gather(gate_act, "cols", axis=0, tiled=True),
        lax.all_gather(up_act, "cols", axis=0, tiled=True),
    )
    weight_grad = lax.dot_general(
        hidden_piece, grads_all, (((0,), (0,)), ((), ())), preferred_element_type=jnp.float32
    )
    return (weight_grad, gate_grad, up_grad)


def solution(mesh):
    in_specs = (P("rows", "cols"), P("cols", "rows"), P("cols", "rows"), P("rows", "cols"))
    out_specs = (P("rows", "cols"), P("cols", "rows"), P("cols", "rows"))
    return jax.shard_map(shards, mesh=mesh, in_specs=in_specs, out_specs=out_specs, check_vma=False)
```

profile of v0, /device:TPU:2, one launch (start us, length us, event | category | flops | bytes accessed | tf_op | source)
XLA Modules:
  0.0 552.3 jit_solution(17468748811259498733)
XLA Ops:
  7.2 0.0 copy-start
  7.2 0.0 all-gather.8.cloned.1.call-start
  7.2 0.7 all-gather.8.cloned.1.call-update
  7.9 0.0 all-gather.4.cloned.1.call-start
  8.0 0.7 all-gather.4.cloned.1.call-update
  8.7 0.0 all-gather.6.cloned.1.call-start
  8.7 0.7 all-gather.6.cloned.1.call-update
  9.4 0.0 reduce-scatter.2.cloned.1.call-start
  9.4 29.3 %all-gather.8.cloned.1.call-done = bf16[2048,256]{1,0:T(8,128)(2,1)} async-done(((bf16[256,256]{1,0:T(8,128)(2,1)}), bf16[2048,256]{1,0:T(8,128)(2,1)}) %all-gather.8.cloned.1.call-update) | async-done | bytes 1048592 | tf_op jit(solution)/shard_map/all_gather | solution.py:15
  38.8 0.0 copy-done
  38.8 8.5 %convolution_convert_fusion = bf16[2048,3584]{1,0:T(8,128)(2,1)} fusion(bf16[2048,256]{1,0:T(8,128)(2,1)} %all-gather.8.cloned.1.call-done, bf16[3584,256]{1,0:T(8,128)(2,1)S(1)} %copy-done), kind=kOutput, calls=%fused_computation.7 | convolution fusion | flops 3765436416 | bytes 17563648 | tf_op jit(solution)/shard_map/dot_general | solution.py:17
  47.3 0.0 reduce-scatter.2.cloned.1.call-update
  47.3 0.0 copy-start.1
  47.4 0.0 copy-start.2
  47.4 122.7 %all-gather.4.cloned.1.call-done = bf16[2048,3584]{1,0:T(8,128)(2,1)} async-done(((bf16[64,3584]{1,0:T(8,128)(2,1)}), bf16[2048,3584]{1,0:T(8,128)(2,1)}) %all-gather.4.cloned.1.call-update) | async-done | bytes 14680080 | tf_op jit(solution)/shard_map/all_gather | solution.py:32
  170.0 129.7 %all-gather.6.cloned.1.call-done = bf16[2048,3584]{1,0:T(8,128)(2,1)} async-done(((bf16[64,3584]{1,0:T(8,128)(2,1)}), bf16[2048,3584]{1,0:T(8,128)(2,1)}) %all-gather.6.cloned.1.call-update) | async-done | bytes 14680080 | tf_op jit(solution)/shard_map/all_gather | solution.py:33
  299.7 16.8 %fusion.5 = f32[3584,256]{1,0:T(8,128)} fusion(bf16[2048,256]{1,0:T(8,128)(2,1)} %all-gather.8.cloned.1.call-done, bf16[2048,3584]{1,0:T(8,128)(2,1)} %all-gather.6.cloned.1.call-done, bf16[2048,3584]{1,0:T(8,128)(2,1)} %all-gather.4.cloned.1.call-done), kind=kOutput, calls=%fused_computation.8 | convolution fusion | flops 3816816640 | bytes 34078720 | tf_op jit(solution)/shard_map/dot_general | solution.py:35
  316.5 226.8 %reduce-scatter.2.cloned.1.call-done = bf16[64,3584]{1,0:T(8,128)(2,1)} async-done(((bf16[2048,3584]{1,0:T(8,128)(2,1)}), bf16[64,3584]{1,0:T(8,128)(2,1)}) %reduce-scatter.2.cloned.1.call-update) | async-done | bytes 458768 | tf_op jit(solution)/shard_map/reduce_scatter | solution.py:16
  543.4 0.0 copy-done.1
  543.4 0.0 copy-done.2
  543.4 2.4 fusion.10
Async XLA Ops:
  7.2 31.6 %copy-start = (bf16[3584,256]{1,0:T(8,128)(2,1)S(1)}, bf16[3584,256]{1,0:T(8,128)(2,1)}, u32[]{:S(2)}) copy-start(bf16[3584,256]{1,0:T(8,128)(2,1)} %param.7) | copy-start | bytes 5505028
  7.2 31.6 %all-gather.8.cloned.1.call-start = ((), (), s32[]{:S(2)}) async-start(), calls=%async_computation.3 | async-start | bytes 1179648 | tf_op jit(solution)/shard_map/all_gather | solution.py:15
  7.9 162.1 %all-gather.4.cloned.1.call-start = ((), (), s32[]{:S(2)}) async-start(), calls=%async_computation.1 | async-start | bytes 15138816 | tf_op jit(solution)/shard_map/all_gather | solution.py:32
  8.7 291.1 %all-gather.6.cloned.1.call-start = ((), (), s32[]{:S(2)}) async-start(), calls=%async_computation.2 | async-start | bytes 15138816 | tf_op jit(solution)/shard_map/all_gather | solution.py:33
  9.4 534.0 %reduce-scatter.2.cloned.1.call-start = ((), (), s32[]{:S(2)}) async-start(), calls=%async_computation.4 | async-start | bytes 15138816 | tf_op jit(solution)/shard_map/reduce_scatter | solution.py:16
  47.3 496.0 %copy-start.1 = (bf16[64,3584]{1,0:T(8,128)(2,1)S(1)}, bf16[64,3584]{1,0:T(8,128)(2,1)}, u32[]{:S(2)}) copy-start(bf16[64,3584]{1,0:T(8,128)(2,1)} %param.5) | copy-start | bytes 1376260
  47.4 496.0 %copy-start.2 = (bf16[64,3584]{1,0:T(8,128)(2,1)S(1)}, bf16[64,3584]{1,0:T(8,128)(2,1)}, u32[]{:S(2)}) copy-start(bf16[64,3584]{1,0:T(8,128)(2,1)} %param.6) | copy-start | bytes 1376260
Sparse Core Ops, SparseCore 0:
  9.9 28.8 all-gather.7
  41.4 128.6 all-gather.3
  172.6 127.0 all-gather.5
  303.8 239.5 reduce-scatter.1
where the time goes:
time: 553 us; the launch traced here: 552 us
  waiting for transfers between devices  511 us (92%)
  matrix products  25.3 us (5%)
  between operations  13.8 us (2%)
    reduce_scatter x1, waiting for transfers between devices, shards(): lax.psum_scatter(lax.dot_general(grads_all, down_weight, (((1,), (1,)), (...  227 us
    all_gather x1, waiting for transfers between devices, shards(): lax.all_gather(up_act, 'cols', axis=0, tiled=True)  130 us
    all_gather x1, waiting for transfers between devices, shards(): lax.all_gather(gate_act, 'cols', axis=0, tiled=True)  123 us
    all_gather x1, waiting for transfers between devices, shards(): grads_all = lax.all_gather(out_grad, 'rows', axis=0, tiled=True)  29.3 us
    dot_general x1, matrix products, shards(): lax.dot_general(hidden_piece, grads_all, (((0,), (0,)), ((), ())), prefer...  16.8 us
  transfers between devices with their start and end apart: 4, of which 4 were waited for; matrix products, arithmetic and copies ran while one was open for 5% of the time, Pallas kernels for 0%

commit v1 on v0

v1 whole, which is shorter than its diff:
```python
import jax
import jax.numpy as jnp
from jax import lax
from jax.experimental import pallas as pl
from jax.experimental.pallas import tpu as pltpu
from jax.sharding import PartitionSpec as P

MESH = pl.DeviceIdType.MESH
NX, NY, NZ = 4, 4, 8
TOK = 64
SUB = 896
DB = 256
DG = NX * DB
BLK = NX * TOK
HALF = BLK // 2
R, L = 0, 1


def kernel(
    g, gate, up, w, hs_out, dw_out,
    gate_v, up_v, hid, hh, hht, gg, wg, part, rs_send, rs_recv, fin, acc, dws,
    lsem, hs_s, hs_r, gx_s, gx_r, gy_s, gy_r, gc_s, gc_r, w_s, w_r,
    ag_s, ag_r, rs_s, rs_r, f_s, f_r, dw_s, dw_r,
):
    r, c = lax.axis_index("rows"), lax.axis_index("cols")
    y, core, x, z = r // 2, r % 2, c // NZ, c % NZ

    def dev(dx=0, dz=0, dy=0, dc=0):
        return (
            ((y + dy) % NY) * 2 + (core + dc) % 2,
            ((x + dx) % NX) * NZ + (z + dz + NZ) % NZ,
        )

    def remote(src, dst, s, d, to):
        return pltpu.make_async_remote_copy(
            src_ref=src, dst_ref=dst, send_sem=s, recv_sem=d, device_id=to, device_id_type=MESH
        )

    def at(i, n):
        return pl.ds(pl.multiple_of(i * n, n), n)

    peers = [dev(dx=1), dev(dx=2), dev(dx=3), dev(dy=1), dev(dy=2), dev(dy=3), dev(dc=1), dev(dz=1), dev(dz=-1)]
    barrier = pltpu.get_barrier_semaphore()
    for peer in peers:
        pl.semaphore_signal(barrier, inc=1, device_id=peer, device_id_type=MESH)

    load_gate = pltpu.make_async_copy(gate, gate_v, lsem.at[0])
    load_up = pltpu.make_async_copy(up, up_v, lsem.at[1])
    load_g = pltpu.make_async_copy(g, gg.at[at(core, 4), at(y, TOK), at(x, DB)], lsem.at[2])
    load_w = pltpu.make_async_copy(w.at[at(x, SUB)], wg.at[:, at(x, DB)], lsem.at[3])
    load_gate.start()
    load_up.start()
    load_g.start()
    load_w.start()
    load_gate.wait()
    load_up.wait()
    for q in range(NX):
        cols = slice(q * SUB, (q + 1) * SUB)
        wide = gate_v[:, cols].astype(jnp.float32)
        swish = wide * jax.nn.sigmoid(wide)
        hid[q] = (swish * up_v[:, cols].astype(jnp.float32)).astype(jnp.bfloat16)
    pl.semaphore_wait(barrier, len(peers))

    sent = []

    def go(copy):
        copy.start()
        sent.append(copy)
        return copy

    hid_copies = []
    for d in (2, 1, 3):
        to = (x + d) % NX
        hid_copies.append(
            go(remote(hid.at[to], hh.at[z, at(x, TOK)], hs_s.at[d - 1], hs_r.at[d - 1], dev(dx=d)))
        )
    hh[z, at(x, TOK)] = hid[x]

    gx_copies = {}
    for d in (2, 1, 3):
        gx_copies[d] = go(
            remote(g, gg.at[at(core, 4), at(y, TOK), at(x, DB)], gx_s.at[d - 1], gx_r.at[d - 1], dev(dx=d))
        )
    load_g.wait()
    gy_copies = {}

    def spread(d):
        src = (x + NX - d) % NX
        piece = gg.at[at(core, 4), at(y, TOK), at(src, DB)]
        for e in (2, 1, 3):
            gy_copies[d, e] = go(remote(piece, piece, gy_s.at[d, e - 1], gy_r.at[d, e - 1], dev(dy=e)))

    spread(0)

    for copy in hid_copies:
        copy.wait_recv()

    def last_hop(way, h):
        return 4 if way == h else 3

    ag_copies = {}

    def ag_send(hop):
        for way in (R, L):
            for h in (way, 1 - way):
                if hop <= last_hop(way, h):
                    b = (z - (hop - 1) + NZ) % NZ if way == R else (z + (hop - 1)) % NZ
                    piece = hh.at[b, h * HALF : (h + 1) * HALF]
                    if hop > 1:
                        ag_copies[way, hop - 1, h].wait_recv()
                    ag_copies[way, hop, h] = go(
                        remote(
                            piece, piece, ag_s.at[way, hop - 1, h], ag_r.at[way, hop - 1, h],
                            dev(dz=1 if way == R else -1),
                        )
                    )

    def turn(b):
        hht[b] = hh[b].T

    ag_send(1)

    w_copies = []
    for d in (2, 1, 3):
        to = (x + d) % NX
        w_copies.append(
            go(remote(w.at[at(to, SUB)], wg.at[:, at(x, DB)], w_s.at[d - 1], w_r.at[d - 1], dev(dx=d)))
        )
    turn(z)

    for d in (1, 3, 2):
        gx_copies[d].wait_recv()
        spread(d)

    ag_send(2)
    turn((z + 1) % NZ)
    turn((z + NZ - 1) % NZ)

    gc_copies = []

    def to_sibling(e):
        rows = gg.at[at(core, 4), at((y + NY - e) % NY, TOK)]
        gc_copies.append(go(remote(rows, rows, gc_s.at[e], gc_r.at[e], dev(dc=1))))

    to_sibling(0)
    for e in (1, 3, 2):
        for d in range(NX):
            gy_copies[d, e].wait_recv()
        to_sibling(e)

    ag_send(3)
    turn((z + 2) % NZ)
    turn((z + NZ - 2) % NZ)

    for copy in gc_copies:
        copy.wait_recv()
    load_w.wait()
    for copy in w_copies:
        copy.wait_recv()

    def multiply(b):
        out = lax.dot_general(gg[b], wg[...], (((1,), (1,)), ((), ())), preferred_element_type=jnp.float32)
        part[b] = out.reshape(NX, TOK, SUB)

    rs_copies = {}

    def rs_send_piece(way, step, h):
        b = (z + 4 - step) % NZ if way == R else (z + 4 + step) % NZ
        value = part[b, :, h * 32 : (h + 1) * 32, :]
        if (way, step - 1, h) in rs_copies:
            rs_copies[way, step - 1, h].wait_recv()
            value = value + rs_recv[way, step - 1, h].astype(jnp.float32)
        rs_send[way, step, h] = value.astype(jnp.bfloat16)
        rs_copies[way, step, h] = go(
            remote(
                rs_send.at[way, step, h], rs_recv.at[way, step, h], rs_s.at[way, step, h], rs_r.at[way, step, h],
                dev(dz=1 if way == R else -1),
            )
        )

    multiply((z + 4) % NZ)
    rs_send_piece(R, 0, 0)
    rs_send_piece(L, 0, 1)

    @pl.loop(0, NZ - 1)
    def _(i):
        multiply((z + 5 + i) % NZ)

    rs_send_piece(R, 1, 1)
    rs_send_piece(L, 1, 0)

    def accumulate(b, first=False):
        @pl.loop(0, NX)
        def _(n):
            cols = at(n, DB)
            out = jnp.dot(hht[b], gg[b, :, cols], preferred_element_type=jnp.float32)
            acc[:, cols] = out if first else acc[:, cols] + out

    accumulate(z, True)

    ag_send(4)
    ag_copies[R, 3, 1].wait_recv()
    ag_copies[L, 3, 0].wait_recv()
    turn((z + 3) % NZ)
    turn((z + NZ - 3) % NZ)

    @pl.loop(0, 3)
    def _(i):
        accumulate((z + 1 + i) % NZ)
        accumulate((z + 7 - i) % NZ)

    ag_copies[R, 4, 0].wait_recv()
    ag_copies[L, 4, 1].wait_recv()
    rs_send_piece(R, 1, 0)
    rs_send_piece(L, 1, 1)
    turn((z + 4) % NZ)
    accumulate((z + 4) % NZ)

    dw_copies = []
    for d in (2, 1, 3):
        to = (x + d) % NX
        dws[to] = acc[:, at(to, DB)].astype(jnp.bfloat16)
        dw_copies.append(go(remote(dws.at[to], dw_out.at[at(x, SUB)], dw_s.at[d - 1], dw_r.at[d - 1], dev(dx=d))))
    dws[x] = acc[:, at(x, DB)].astype(jnp.bfloat16)
    keep_dw = pltpu.make_async_copy(dws.at[x], dw_out.at[at(x, SUB)], lsem.at[4])
    keep_dw.start()

    for step in (2, 3):
        for h in (1, 0):
            rs_send_piece(R, step, h)
            rs_send_piece(L, step, 1 - h)

    f_copies, keep = [], []
    for h in range(2):
        value = part[z, :, h * 32 : (h + 1) * 32, :]
        for way in (R, L):
            rs_copies[way, 3, h].wait_recv()
            value = value + rs_recv[way, 3, h].astype(jnp.float32)
        fin[h] = value.astype(jnp.bfloat16)
        rows = hs_out.at[h * 32 : (h + 1) * 32, pl.ds(pl.multiple_of(x * SUB, 128), SUB)]
        for d in (2, 1, 3):
            to = (x + d) % NX
            f_copies.append(go(remote(fin.at[h, to], rows, f_s.at[h, d - 1], f_r.at[h, d - 1], dev(dx=d))))
        keep.append(pltpu.make_async_copy(fin.at[h, x], rows, lsem.at[5 + h]))
        keep[-1].start()

    keep_dw.wait()
    for copy in keep:
        copy.wait()
    for copy in dw_copies:
        copy.wait_recv()
    for copy in f_copies:
        copy.wait_recv()
    for copy in sent:
        copy.wait_send()


def shards(out_grad, gate_act, up_act, down_weight):
    bf, dma = jnp.bfloat16, pltpu.SemaphoreType.DMA
    anywhere = pl.BlockSpec(memory_space=pl.ANY)
    hidden_grad, grad = pl.pallas_call(
        kernel,
        out_shape=(
            jax.ShapeDtypeStruct((TOK, NX * SUB), bf),
            jax.ShapeDtypeStruct((NX * SUB, DB), bf),
        ),
        in_specs=[anywhere] * 4,
        out_specs=(anywhere, anywhere),
        scratch_shapes=[
            pltpu.VMEM((TOK, NX * SUB), bf),
            pltpu.VMEM((TOK, NX * SUB), bf),
            pltpu.VMEM((NX, TOK, SUB), bf),
            pltpu.VMEM((NZ, BLK, SUB), bf),
            pltpu.VMEM((NZ, SUB, BLK), bf),
            pltpu.VMEM((NZ, BLK, DG), bf),
            pltpu.VMEM((SUB, DG), bf),
            pltpu.VMEM((NZ, NX, TOK, SUB), jnp.float32),
            pltpu.VMEM((2, 4, 2, NX, 32, SUB), bf),
            pltpu.VMEM((2, 4, 2, NX, 32, SUB), bf),
            pltpu.VMEM((2, NX, 32, SUB), bf),
            pltpu.VMEM((SUB, DG), jnp.float32),
            pltpu.VMEM((NX, SUB, DB), bf),
            dma((7,)),
            dma((3,)), dma((3,)),
            dma((3,)), dma((3,)),
            dma((4, 3)), dma((4, 3)),
            dma((4,)), dma((4,)),
            dma((3,)), dma((3,)),
            dma((2, 4, 2)), dma((2, 4, 2)),
            dma((2, 4, 2)), dma((2, 4, 2)),
            dma((2, 3)), dma((2, 3)),
            dma((3,)), dma((3,)),
        ],
        compiler_params=pltpu.CompilerParams(
            collective_id=0, has_side_effects=True, vmem_limit_bytes=52 << 20
        ),
    )(out_grad.reshape(4, TOK, DB), gate_act, up_act, down_weight)
    hidden_grad = hidden_grad.astype(jnp.float32)
    gate_wide = gate_act.astype(jnp.float32)
    up_wide = up_act.astype(jnp.float32)
    sigmoid_gate = jax.nn.sigmoid(gate_wide)
    gate_grad = hidden_grad * up_wide * sigmoid_gate * (1.0 + gate_wide * (1.0 - sigmoid_gate))
    up_grad = hidden_grad * (gate_wide * sigmoid_gate)
    return grad.astype(jnp.float32), gate_grad.astype(jnp.bfloat16), up_grad.astype(jnp.bfloat16)


def solution(mesh):
    in_specs = (P("rows", "cols"), P("cols", "rows"), P("cols", "rows"), P("rows", "cols"))
    out_specs = (P("rows", "cols"), P("cols", "rows"), P("cols", "rows"))
    return jax.shard_map(shards, mesh=mesh, in_specs=in_specs, out_specs=out_specs, check_vma=False)
```

time: 553 us -> 108 us (0.20)
  waiting for transfers between devices: 511 us -> 0 us
  Pallas kernels: 0 us -> 98.9 us
  matrix products: 25.3 us -> 0 us
  between operations: 13.8 us -> 0.65 us
    all_gather x3 -> x0, waiting for transfers between devices: 282 us -> none  [the longest x1 130 us: shards(): lax.all_gather(up_act, 'cols', axis=0, tiled=True)]
    reduce_scatter x1 -> x0, waiting for transfers between devices: 227 us -> none  [shards(): lax.psum_scatter(lax.dot_general(grads_all, down_weight, (((1,), (1,)), (...]
    pallas_call x0 -> x1, Pallas kernels: none -> 98.9 us  [shards(): pl.pallas_call(kernel, out_shape=(jax.ShapeDtypeStruct((TOK, NX * SUB), b...]
    dot_general x2 -> x0, matrix products: 25.3 us -> none  [the longest x1 16.8 us: shards(): lax.dot_general(hidden_piece, grads_all, (((0,), (0,)), ((), ())), prefer...]
  transfers between devices with their start and end apart: 4 -> 0, of which waited for: 4 -> 0; matrix products, arithmetic and copies ran while one was open for 5% -> 0% of each run, Pallas kernels for 0% -> 0%
where the time goes in v1:
time: 108 us; the launch traced here: 107 us
  Pallas kernels  98.9 us (92%)
  other arithmetic  5.02 us (5%)
  local copies, waits for them, and re-layouts  2.93 us (3%)
    pallas_call x1, Pallas kernels, shards(): pl.pallas_call(kernel, out_shape=(jax.ShapeDtypeStruct((TOK, NX * SUB), b...  98.9 us
    convert_element_type x1, other arithmetic, shards(): grad.astype(jnp.float32)  3.62 us
    unnamed x6, local copies, waits for them, and re-layouts  2.93 us

profile of v1, /device:TPU:2, one launch (start us, length us, event | category | flops | bytes accessed | tf_op | source)
XLA Modules:
  0.0 107.5 jit_solution(1784822478757590157)
XLA Ops:
  0.6 0.0 copy-start
  0.6 1.0 copy-done
  1.7 0.0 copy-start.1
  1.7 1.0 copy-done.1
  2.7 0.0 copy-start.2
  2.7 0.9 copy-done.2
  3.6 98.9 %shard_map.67 = (bf16[64,3584]{1,0:T(8,128)(2,1)S(1)}, bf16[3584,256]{1,0:T(8,128)(2,1)}) custom-call(bf16[4,64,256]{2,1,0:T(8,128)(2,1)S(1)} %bitcast.1, bf16[64,3584]{1,0:T(8,128)(2,1)S(1)} %copy-done, bf16[64,3584]{1,0:T(8,128)(2,1)S(1)} %copy-done.1, bf16[3584,256]{1,0:T(8,128)(2,1)} %w.1), custom_call_target="tpu_custom_call" | custom-call | tf_op jit(solution)/shard_map/pallas_call | solution.py:261
  102.5 3.6 %convert_element_type.18 = f32[3584,256]{1,0:T(8,128)} convert(bf16[3584,256]{1,0:T(8,128)(2,1)} %get-tuple-element.5) | non-fusion elementwise | flops 917504 | bytes 5505024 | tf_op jit(solution)/shard_map/convert_element_type | solution.py:304
  106.1 1.4 %fusion.3 = (bf16[64,3584]{1,0:T(8,128)(2,1)}, bf16[64,3584]{1,0:T(8,128)(2,1)}) fusion(bf16[64,3584]{1,0:T(8,128)(2,1)S(1)} %get-tuple-element.6, bf16[64,3584]{1,0:T(8,128)(2,1)S(1)} %copy-done, bf16[64,3584]{1,0:T(8,128)(2,1)S(1)} %copy-done.1), kind=kLoop, calls=%fused_computation.8 | loop fusion | flops 3670016 | bytes 2293760 | tf_op jit(solution)/shard_map/convert_element_type | solution.py:304
Async XLA Ops:
  0.6 1.0 copy-start
  1.7 1.0 copy-start.1
  2.7 0.9 copy-start.2

commit v2 on v0

v2 whole, which is shorter than its diff:
```python
import jax
import jax.numpy as jnp
from jax import lax
from jax.experimental import pallas as pl
from jax.experimental.pallas import tpu as pltpu
from jax.sharding import PartitionSpec as P

MESH = pl.DeviceIdType.MESH
NX, NY, NZ = 4, 4, 8
TOK = 64
SUB = 896
DB = 256
DG = NX * DB
BLK = NX * TOK
Q = 16
NQ = TOK // Q
R, L = 0, 1
F32, BF16 = jnp.float32, jnp.bfloat16


def kernel(
    g, gate, up, w, dw_out, gate_out, up_out,
    gate_v, up_v, hid, hh, gg, wg, part, rs_send, rs_recv, fin, fbuf, gate_f, up_f, acc, dws, land,
    lsem, hs_s, hs_r, gx_s, gx_r, gy_s, gy_r, gc_s, gc_r, w_s, w_r,
    ag_s, ag_r, rs_s, rs_r, f_s, f_r, dw_s, dw_r,
):
    r, c = lax.axis_index("rows"), lax.axis_index("cols")
    y, core, x, z = r // 2, r % 2, c // NZ, c % NZ

    def dev(dx=0, dz=0, dy=0, dc=0):
        return (
            ((y + dy) % NY) * 2 + (core + dc) % 2,
            ((x + dx) % NX) * NZ + (z + dz + NZ) % NZ,
        )

    sent = []

    def send(src, dst, s, d, to):
        copy = pltpu.make_async_remote_copy(
            src_ref=src, dst_ref=dst, send_sem=s, recv_sem=d, device_id=to, device_id_type=MESH
        )
        copy.start()
        sent.append(copy)
        return copy

    def at(i, n):
        return pl.ds(pl.multiple_of(i * n, n), n)

    def lanes(i):
        return pl.ds(pl.multiple_of(i * SUB, 128), SUB)

    peers = [dev(dx=1), dev(dx=2), dev(dx=3), dev(dy=1), dev(dy=2), dev(dy=3), dev(dc=1), dev(dz=1), dev(dz=-1)]
    barrier = pltpu.get_barrier_semaphore()
    for peer in peers:
        pl.semaphore_signal(barrier, inc=1, device_id=peer, device_id_type=MESH)

    load_gate = pltpu.make_async_copy(gate, gate_v, lsem.at[0])
    load_up = pltpu.make_async_copy(up, up_v, lsem.at[1])
    load_g = pltpu.make_async_copy(g, gg.at[at(core, 4), at(y, TOK), at(x, DB)], lsem.at[2])
    load_w = pltpu.make_async_copy(w.at[at(x, SUB)], wg.at[:, at(x, DB)], lsem.at[3])
    load_gate.start()
    load_up.start()
    load_g.start()
    load_w.start()
    load_gate.wait()
    load_up.wait()
    for d in (0, 1, 3, 2):
        to = (x + d) % NX
        wide = gate_v[:, lanes(to)].astype(F32)
        swish = wide * jax.nn.sigmoid(wide)
        value = (swish * up_v[:, lanes(to)].astype(F32)).astype(BF16)
        if d == 0:
            hh[z, at(x, TOK)] = value
        else:
            hid[to] = value
    load_g.wait()
    pl.semaphore_wait(barrier, len(peers))

    ag = {}

    def last_hop(way, d):
        return 4 if (way == R) == (d < 2) else 3

    def gather(hop, d):
        src = (x + NX - d) % NX
        for way in (R, L):
            if hop > 1 and hop - 1 <= last_hop(way, d):
                ag[way, hop - 1, d].wait_recv()
            if hop <= last_hop(way, d):
                b = (z - (hop - 1) + NZ) % NZ if way == R else (z + (hop - 1)) % NZ
                piece = hh.at[b, at(src, TOK)]
                ag[way, hop, d] = send(
                    piece, piece, ag_s.at[way, hop - 1, d], ag_r.at[way, hop - 1, d], dev(dz=1 if way == R else -1)
                )

    gather(1, 0)

    hid_copies = {}
    for d in (1, 3, 2):
        to = (x + d) % NX
        hid_copies[d] = send(hid.at[to], hh.at[z, at(x, TOK)], hs_s.at[d - 1], hs_r.at[d - 1], dev(dx=d))

    gy = {}

    def spread(d):
        src = (x + NX - d) % NX
        piece = gg.at[at(core, 4), at(y, TOK), at(src, DB)]
        for e in (1, 3, 2):
            gy[d, e] = send(piece, piece, gy_s.at[d, e - 1], gy_r.at[d, e - 1], dev(dy=e))

    spread(0)
    for d in (1, 3):
        hid_copies[d].wait_recv()
        gather(1, d)
    gx = {}
    for d in (1, 3, 2):
        gx[d] = send(g, gg.at[at(core, 4), at(y, TOK), at(x, DB)], gx_s.at[d - 1], gx_r.at[d - 1], dev(dx=d))
    hid_copies[2].wait_recv()
    gather(1, 2)
    w_copies = []
    for d in (1, 3, 2):
        to = (x + d) % NX
        w_copies.append(send(w.at[at(to, SUB)], wg.at[:, at(x, DB)], w_s.at[d - 1], w_r.at[d - 1], dev(dx=d)))

    gather(2, 0)
    for d in (1, 3):
        gx[d].wait_recv()
        spread(d)
    gather(2, 1)
    gx[2].wait_recv()
    spread(2)

    gc = []

    def to_sibling(e):
        rows = gg.at[at(core, 4), at((y + NY - e) % NY, TOK)]
        gc.append(send(rows, rows, gc_s.at[e], gc_r.at[e], dev(dc=1)))

    to_sibling(0)
    gather(2, 3)
    gather(2, 2)

    for i in range(NX):
        cols = slice(i * SUB, (i + 1) * SUB)
        wide = gate_v[:, cols].astype(F32)
        sigmoid = jax.nn.sigmoid(wide)
        gate_f[:, cols] = up_v[:, cols].astype(F32) * sigmoid * (1.0 + wide * (1.0 - sigmoid))
        up_f[:, cols] = wide * sigmoid

    for d in (0, 1, 3, 2):
        gather(3, d)
    for e in (1, 3, 2):
        for d in (0, 1, 3, 2):
            gy[d, e].wait_recv()
        to_sibling(e)
    gather(4, 0)
    for copy in gc:
        copy.wait_recv()

    def product(b):
        return lax.dot_general(hh[b], gg[b], (((0,), (0,)), ((), ())), preferred_element_type=F32)

    acc[...] = product(z)

    @pl.loop(0, 2)
    def _(i):
        acc[...] += product((z + 1 + 6 * i) % NZ)

    gather(4, 1)
    load_w.wait()
    for copy in w_copies:
        copy.wait_recv()

    def multiply(b):
        out = lax.dot_general(gg[b], wg[...], (((1,), (1,)), ((), ())), preferred_element_type=F32)
        part[b] = out.reshape(NX, TOK, SUB)

    rs = {}

    def pieces(way, step):
        first, second = ((2, 3), (0, 1)) if way == R else ((0, 1), (2, 3))
        return second if step == 0 else first + second

    def reduce(way, step, k):
        b = (z + 4 - step) % NZ if way == R else (z + 4 + step) % NZ
        value = part[b, :, k * Q : (k + 1) * Q, :]
        if (way, step - 1, k) in rs:
            rs[way, step - 1, k].wait_recv()
            value = value + rs_recv[way, step - 1, k].astype(F32)
        rs_send[way, step, k] = value.astype(BF16)
        rs[way, step, k] = send(
            rs_send.at[way, step, k], rs_recv.at[way, step, k], rs_s.at[way, step, k], rs_r.at[way, step, k],
            dev(dz=1 if way == R else -1),
        )

    def reduce_both(step, ks):
        for i in ks:
            for way in (R, L):
                reduce(way, step, pieces(way, step)[i])

    multiply((z + 4) % NZ)
    reduce_both(0, (0, 1))
    gather(4, 3)
    multiply((z + 3) % NZ)
    multiply((z + 5) % NZ)
    reduce_both(1, (0, 1))
    gather(4, 2)

    @pl.loop(0, 5)
    def _(i):
        multiply((z + 6 + i) % NZ)

    @pl.loop(0, 2)
    def _(i):
        acc[...] += product((z + 2 + 4 * i) % NZ)

    reduce_both(1, (2, 3))

    @pl.loop(0, 2)
    def _(i):
        acc[...] += product((z + 3 + 2 * i) % NZ)

    for way, d in ((R, 0), (R, 1), (L, 3), (L, 2)):
        ag[way, 4, d].wait_recv()
    last = (z + 4) % NZ
    dw = {}
    for d in (1, 3, 2, 0):
        to = (x + d) % NX
        total = acc[:, at(to, DB)] + lax.dot_general(
            hh[last], gg[last, :, at(to, DB)], (((0,), (0,)), ((), ())), preferred_element_type=F32
        )
        if d == 0:
            dw_out[at(x, SUB)] = total
        else:
            dws[to] = total.astype(BF16)
            dw[d] = send(dws.at[to], land.at[x], dw_s.at[d - 1], dw_r.at[d - 1], dev(dx=d))

    reduce_both(2, (0, 1, 2, 3))
    reduce_both(3, (0, 1, 2, 3))
    for d in (1, 3, 2):
        dw[d].wait_recv()
        src = (x + NX - d) % NX
        dw_out[at(src, SUB)] = land[src].astype(F32)

    f = {}
    for k in (2, 0, 3, 1):
        rows = slice(k * Q, (k + 1) * Q)
        value = part[z, :, rows, :]
        for way in (R, L):
            rs[way, 3, k].wait_recv()
            value = value + rs_recv[way, 3, k].astype(F32)
        fin[k] = value.astype(BF16)
        for d in (1, 3, 2):
            to = (x + d) % NX
            f[k, d] = send(fin.at[k, to], fbuf.at[x, rows], f_s.at[k, d - 1], f_r.at[k, d - 1], dev(dx=d))
    for k in (2, 0, 3, 1):
        rows = slice(k * Q, (k + 1) * Q)
        for d in (0, 1, 3, 2):
            src = (x + NX - d) % NX
            if d == 0:
                value = fin[k, x].astype(F32)
            else:
                f[k, d].wait_recv()
                value = fbuf[src, rows].astype(F32)
            gate_out[rows, lanes(src)] = (value * gate_f[rows, lanes(src)]).astype(BF16)
            up_out[rows, lanes(src)] = (value * up_f[rows, lanes(src)]).astype(BF16)

    for copy in sent:
        copy.wait_send()


def copy_out(*refs):
    ins, outs, sems = refs[:3], refs[3:6], refs[6]
    copies = [pltpu.make_async_copy(ins[i], outs[i], sems.at[i]) for i in range(3)]
    for copy in copies:
        copy.start()
    for copy in copies:
        copy.wait()


def shards(out_grad, gate_act, up_act, down_weight):
    dma = pltpu.SemaphoreType.DMA
    anywhere = pl.BlockSpec(memory_space=pl.ANY)
    in_vmem = pl.BlockSpec(memory_space=pltpu.VMEM)
    shapes = [((NX * SUB, DB), F32), ((TOK, NX * SUB), BF16), ((TOK, NX * SUB), BF16)]
    operands = (out_grad.reshape(4, TOK, DB), gate_act, up_act, down_weight)
    results = pl.pallas_call(
        kernel,
        out_shape=[pltpu.VMEM(*shape) for shape in shapes],
        in_specs=[anywhere] * 4,
        out_specs=[in_vmem] * 3,
        scratch_shapes=[
            pltpu.VMEM((TOK, NX * SUB), BF16),
            pltpu.VMEM((TOK, NX * SUB), BF16),
            pltpu.VMEM((NX, TOK, SUB), BF16),
            pltpu.VMEM((NZ, BLK, SUB), BF16),
            pltpu.VMEM((NZ, BLK, DG), BF16),
            pltpu.VMEM((SUB, DG), BF16),
            pltpu.VMEM((NZ, NX, TOK, SUB), F32),
            pltpu.VMEM((2, 4, NQ, NX, Q, SUB), BF16),
            pltpu.VMEM((2, 4, NQ, NX, Q, SUB), BF16),
            pltpu.VMEM((NQ, NX, Q, SUB), BF16),
            pltpu.VMEM((NX, TOK, SUB), BF16),
            pltpu.VMEM((TOK, NX * SUB), F32),
            pltpu.VMEM((TOK, NX * SUB), F32),
            pltpu.VMEM((SUB, DG), F32),
            pltpu.VMEM((NX, SUB, DB), BF16),
            pltpu.VMEM((NX, SUB, DB), BF16),
            dma((4,)),
            dma((3,)), dma((3,)),
            dma((3,)), dma((3,)),
            dma((4, 3)), dma((4, 3)),
            dma((4,)), dma((4,)),
            dma((3,)), dma((3,)),
            dma((2, 4, 4)), dma((2, 4, 4)),
            dma((2, 4, NQ)), dma((2, 4, NQ)),
            dma((NQ, 3)), dma((NQ, 3)),
            dma((3,)), dma((3,)),
        ],
        compiler_params=pltpu.CompilerParams(
            collective_id=0, has_side_effects=True, vmem_limit_bytes=50 << 20
        ),
    )(*[pltpu.with_memory_space_constraint(operand, pltpu.HBM) for operand in operands])
    return pl.pallas_call(
        copy_out,
        out_shape=[jax.ShapeDtypeStruct(*shape) for shape in shapes],
        in_specs=[anywhere] * 3,
        out_specs=[anywhere] * 3,
        scratch_shapes=[dma((3,))],
        compiler_params=pltpu.CompilerParams(vmem_limit_bytes=1 << 20),
    )(*[pltpu.with_memory_space_constraint(result, pltpu.VMEM) for result in results])


def solution(mesh):
    in_specs = (P("rows", "cols"), P("cols", "rows"), P("cols", "rows"), P("rows", "cols"))
    out_specs = (P("rows", "cols"), P("cols", "rows"), P("cols", "rows"))
    return jax.shard_map(shards, mesh=mesh, in_specs=in_specs, out_specs=out_specs, check_vma=False)
```

time: 553 us -> 91.9 us (0.17)
  the two profiles are of different devices: /device:TPU:2 before, /device:TPU:64 now
where the time goes in v2:
time: 91.9 us; the launch traced here: 91.8 us
  Pallas kernels  91.1 us (99%)
    pallas_call x1, Pallas kernels, shards(): pl.pallas_call(kernel, out_shape=[pltpu.VMEM(*shape) for shape in shapes]...  89 us
    pallas_call x1, Pallas kernels, shards(): pl.pallas_call(copy_out, out_shape=[jax.ShapeDtypeStruct(*shape) for shap...  2.15 us

profile of v2, /device:TPU:64, one launch (start us, length us, event | category | flops | bytes accessed | tf_op | source)
XLA Modules:
  0.0 91.8 jit_solution(3983151690084146555)
XLA Ops:
  0.6 89.0 %shard_map.67 = (f32[3584,256]{1,0:T(8,128)S(1)}, bf16[64,3584]{1,0:T(8,128)(2,1)S(1)}, bf16[64,3584]{1,0:T(8,128)(2,1)S(1)}) custom-call(bf16[4,64,256]{2,1,0:T(8,128)(2,1)} %bitcast.1, bf16[64,3584]{1,0:T(8,128)(2,1)} %gate.1, bf16[64,3584]{1,0:T(8,128)(2,1)} %up.1, bf16[3584,256]{1,0:T(8,128)(2,1)} %w.1), custom_call_target="tpu_custom_call" | custom-call | tf_op jit(solution)/shard_map/pallas_call | solution.py:287
  89.6 2.2 %shard_map.68 = (f32[3584,256]{1,0:T(8,128)}, bf16[64,3584]{1,0:T(8,128)(2,1)}, bf16[64,3584]{1,0:T(8,128)(2,1)}) custom-call(f32[3584,256]{1,0:T(8,128)S(1)} %get-tuple-element.6.refs_0_, bf16[64,3584]{1,0:T(8,128)(2,1)S(1)} %get-tuple-element.7.refs_1_, bf16[64,3584]{1,0:T(8,128)(2,1)S(1)} %get-tuple-element.8.refs_2_), custom_call_target="tpu_custom_call" | custom-call | tf_op jit(solution)/shard_map/pallas_call | solution.py:324

commit v3 on v2

--- a/solution.py
+++ b/solution.py
@@ -20,9 +20,9 @@
 
 def kernel(
     g, gate, up, w, dw_out, gate_out, up_out,
-    gate_v, up_v, hid, hh, gg, wg, part, rs_send, rs_recv, fin, fbuf, gate_f, up_f, acc, dws, land,
-    lsem, hs_s, hs_r, gx_s, gx_r, gy_s, gy_r, gc_s, gc_r, w_s, w_r,
-    ag_s, ag_r, rs_s, rs_r, f_s, f_r, dw_s, dw_r,
+    gate_v, up_v, hid, hh, gg, wg, part, rs_send, rs_recv, fin, fbuf, gate_f, up_f, acc, dws, land, x_land,
+    act_sem, lsem, hs_s, hs_r, gx_s, gx_r, gy_s, gy_r, gc_s, gc_r, w_s, w_r,
+    ag_s, ag_r, rs_s, rs_r, f_s, f_r, x_s, x_r, dw_s, dw_r,
 ):
     r, c = lax.axis_index("rows"), lax.axis_index("cols")
     y, core, x, z = r // 2, r % 2, c // NZ, c % NZ
@@ -43,6 +43,11 @@
         sent.append(copy)
         return copy
 
+    def drain(count):
+        for copy in sent[:count]:
+            copy.wait_send()
+        del sent[:count]
+
     def at(i, n):
         return pl.ds(pl.multiple_of(i * n, n), n)
 
@@ -54,26 +59,26 @@
     for peer in peers:
         pl.semaphore_signal(barrier, inc=1, device_id=peer, device_id_type=MESH)
 
-    load_gate = pltpu.make_async_copy(gate, gate_v, lsem.at[0])
-    load_up = pltpu.make_async_copy(up, up_v, lsem.at[1])
-    load_g = pltpu.make_async_copy(g, gg.at[at(core, 4), at(y, TOK), at(x, DB)], lsem.at[2])
-    load_w = pltpu.make_async_copy(w.at[at(x, SUB)], wg.at[:, at(x, DB)], lsem.at[3])
-    load_gate.start()
-    load_up.start()
+    loads = {}
+    for d in (0, 1, 3, 2):
+        cols = lanes((x + d) % NX)
+        for i, (src, dst) in enumerate(((gate, gate_v), (up, up_v))):
+            loads[d, i] = pltpu.make_async_copy(src.at[:, cols], dst.at[:, cols], act_sem.at[d, i])
+            loads[d, i].start()
+    load_g = pltpu.make_async_copy(g, gg.at[at(core, 4), at(y, TOK), at(x, DB)], lsem.at[0])
+    load_w = pltpu.make_async_copy(w.at[at(x, SUB)], wg.at[:, at(x, DB)], lsem.at[1])
     load_g.start()
     load_w.start()
-    load_gate.wait()
-    load_up.wait()
-    for d in (0, 1, 3, 2):
-        to = (x + d) % NX
-        wide = gate_v[:, lanes(to)].astype(F32)
+
+    def hidden(d):
+        loads[d, 0].wait()
+        loads[d, 1].wait()
+        cols = lanes((x + d) % NX)
+        wide = gate_v[:, cols].astype(F32)
         swish = wide * jax.nn.sigmoid(wide)
-        value = (swish * up_v[:, lanes(to)].astype(F32)).astype(BF16)
-        if d == 0:
-            hh[z, at(x, TOK)] = value
-        else:
-            hid[to] = value
-    load_g.wait()
+        return (swish * up_v[:, cols].astype(F32)).astype(BF16)
+
+    hh[z, at(x, TOK)] = hidden(0)
     pl.semaphore_wait(barrier, len(peers))
 
     ag = {}
@@ -98,16 +103,37 @@
     hid_copies = {}
     for d in (1, 3, 2):
         to = (x + d) % NX
+        hid[to] = hidden(d)
         hid_copies[d] = send(hid.at[to], hh.at[z, at(x, TOK)], hs_s.at[d - 1], hs_r.at[d - 1], dev(dx=d))
 
-    gy = {}
+    gy, gc = {}, []
+
+    def rows_of(d, e, first=0, n=4):
+        src = (x + NX - d) % NX
+        return gg.at[pl.ds(core * 4 + first, n), at((y + NY - e) % NY, TOK), at(src, DB)]
+
+    def to_sibling(d, i, piece):
+        gc.append(send(piece, piece, gc_s.at[d, i], gc_r.at[d, i], dev(dc=1)))
 
     def spread(d):
-        src = (x + NX - d) % NX
-        piece = gg.at[at(core, 4), at(y, TOK), at(src, DB)]
-        for e in (1, 3, 2):
-            gy[d, e] = send(piece, piece, gy_s.at[d, e - 1], gy_r.at[d, e - 1], dev(dy=e))
-
+        piece = rows_of(d, 0)
+        for i, e in enumerate((1, 3)):
+            gy[d, i] = send(piece, piece, gy_s.at[d, i], gy_r.at[d, i], dev(dy=e))
+        to_sibling(d, 4, piece)
+
+    def relay(d):
+        for i, e in enumerate((1, 3)):
+            gy[d, i].wait_recv()
+            half = rows_of(d, e, 2 * i, 2)
+            gy[d, 2 + i] = send(half, half, gy_s.at[d, 2 + i], gy_r.at[d, 2 + i], dev(dy=e))
+            to_sibling(d, i, rows_of(d, e))
+
+    def finish(d):
+        for i in range(2):
+            gy[d, 2 + i].wait_recv()
+            to_sibling(d, 2 + i, rows_of(d, 2, 2 * i, 2))
+
+    load_g.wait()
     spread(0)
     for d in (1, 3):
         hid_copies[d].wait_recv()
@@ -121,23 +147,15 @@
     for d in (1, 3, 2):
         to = (x + d) % NX
         w_copies.append(send(w.at[at(to, SUB)], wg.at[:, at(x, DB)], w_s.at[d - 1], w_r.at[d - 1], dev(dx=d)))
-
     gather(2, 0)
+    relay(0)
+    gather(2, 1)
     for d in (1, 3):
         gx[d].wait_recv()
         spread(d)
-    gather(2, 1)
+    gather(2, 3)
     gx[2].wait_recv()
     spread(2)
-
-    gc = []
-
-    def to_sibling(e):
-        rows = gg.at[at(core, 4), at((y + NY - e) % NY, TOK)]
-        gc.append(send(rows, rows, gc_s.at[e], gc_r.at[e], dev(dc=1)))
-
-    to_sibling(0)
-    gather(2, 3)
     gather(2, 2)
 
     for i in range(NX):
@@ -147,13 +165,17 @@
         gate_f[:, cols] = up_v[:, cols].astype(F32) * sigmoid * (1.0 + wide * (1.0 - sigmoid))
         up_f[:, cols] = wide * sigmoid
 
-    for d in (0, 1, 3, 2):
-        gather(3, d)
-    for e in (1, 3, 2):
-        for d in (0, 1, 3, 2):
-            gy[d, e].wait_recv()
-        to_sibling(e)
-    gather(4, 0)
+    relay(1)
+    gather(3, 0)
+    relay(3)
+    finish(0)
+    gather(3, 1)
+    relay(2)
+    finish(1)
+    gather(3, 3)
+    finish(3)
+    gather(3, 2)
+    finish(2)
     for copy in gc:
         copy.wait_recv()
 
@@ -166,7 +188,20 @@
     def _(i):
         acc[...] += product((z + 1 + 6 * i) % NZ)
 
+    gather(4, 0)
+
+    @pl.loop(0, 2)
+    def _(i):
+        acc[...] += product((z + 2 + 4 * i) % NZ)
+
     gather(4, 1)
+    gather(4, 3)
+    gather(4, 2)
+
+    @pl.loop(0, 2)
+    def _(i):
+        acc[...] += product((z + 3 + 2 * i) % NZ)
+
     load_w.wait()
     for copy in w_copies:
         copy.wait_recv()
@@ -177,48 +212,55 @@
 
     rs = {}
 
-    def pieces(way, step):
-        first, second = ((2, 3), (0, 1)) if way == R else ((0, 1), (2, 3))
-        return second if step == 0 else first + second
-
-    def reduce(way, step, k):
+    order = {
+        R: ((1, 0), (3, 2, 1, 0), (3, 1, 2, 0), (2, 0)),
+        L: ((3, 2), (1, 0, 3, 2), (1, 3, 0, 2), (0, 2)),
+    }
+
+    def running(way, step, k):
         b = (z + 4 - step) % NZ if way == R else (z + 4 + step) % NZ
         value = part[b, :, k * Q : (k + 1) * Q, :]
         if (way, step - 1, k) in rs:
             rs[way, step - 1, k].wait_recv()
             value = value + rs_recv[way, step - 1, k].astype(F32)
-        rs_send[way, step, k] = value.astype(BF16)
+        return value.astype(BF16)
+
+    def pass_on(way, step, k, src):
         rs[way, step, k] = send(
-            rs_send.at[way, step, k], rs_recv.at[way, step, k], rs_s.at[way, step, k], rs_r.at[way, step, k],
-            dev(dz=1 if way == R else -1),
+            src, rs_recv.at[way, step, k], rs_s.at[way, step, k], rs_r.at[way, step, k], dev(dz=1 if way == R else -1)
         )
 
-    def reduce_both(step, ks):
-        for i in ks:
+    def reduce_both(step, places):
+        for i in places:
             for way in (R, L):
-                reduce(way, step, pieces(way, step)[i])
+                k = order[way][step][i]
+                rs_send[way, step, k] = running(way, step, k)
+                pass_on(way, step, k, rs_send.at[way, step, k])
+
+    early = (3, 1)
+    swapped = {}
+
+    def swap(who, k, src):
+        i = early.index(k)
+        for d in (1, 3, 2):
+            swapped[who, k, d] = send(
+                src.at[(x + d) % NX], x_land.at[who, i, x], x_s.at[who, i, d - 1], x_r.at[who, i, d - 1], dev(dx=d)
+            )
+        x_land[who, i, x] = src[x]
+
+    def wait_swap(who, k):
+        for d in (1, 3, 2):
+            swapped[who, k, d].wait_recv()
 
     multiply((z + 4) % NZ)
     reduce_both(0, (0, 1))
-    gather(4, 3)
     multiply((z + 3) % NZ)
     multiply((z + 5) % NZ)
     reduce_both(1, (0, 1))
-    gather(4, 2)
 
     @pl.loop(0, 5)
     def _(i):
         multiply((z + 6 + i) % NZ)
-
-    @pl.loop(0, 2)
-    def _(i):
-        acc[...] += product((z + 2 + 4 * i) % NZ)
-
-    reduce_both(1, (2, 3))
-
-    @pl.loop(0, 2)
-    def _(i):
-        acc[...] += product((z + 3 + 2 * i) % NZ)
 
     for way, d in ((R, 0), (R, 1), (L, 3), (L, 2)):
         ag[way, 4, d].wait_recv()
@@ -235,15 +277,32 @@
             dws[to] = total.astype(BF16)
             dw[d] = send(dws.at[to], land.at[x], dw_s.at[d - 1], dw_r.at[d - 1], dev(dx=d))
 
+    before = len(sent) - 11
+    reduce_both(1, (2, 3))
+    drain(before)
+    before = len(sent)
     reduce_both(2, (0, 1, 2, 3))
-    reduce_both(3, (0, 1, 2, 3))
+    drain(before)
+    before = len(sent)
+    for way, k in ((R, 3), (L, 1), (R, 1), (L, 3)):
+        rs_send[way, 3, k] = running(way, 3, k)
+        swap(way, k, rs_send.at[way, 3, k])
+    for k in early:
+        fin[k] = part[z, :, k * Q : (k + 1) * Q, :].astype(BF16)
+        swap(2, k, fin.at[k])
+    reduce_both(3, (0, 1))
+    for k in early:
+        for way in (R, L):
+            wait_swap(way, k)
+            pass_on(way, 3, k, x_land.at[way, early.index(k)])
+    drain(before)
     for d in (1, 3, 2):
         dw[d].wait_recv()
         src = (x + NX - d) % NX
         dw_out[at(src, SUB)] = land[src].astype(F32)
 
     f = {}
-    for k in (2, 0, 3, 1):
+    for i, k in enumerate((2, 0)):
         rows = slice(k * Q, (k + 1) * Q)
         value = part[z, :, rows, :]
         for way in (R, L):
@@ -252,21 +311,30 @@
         fin[k] = value.astype(BF16)
         for d in (1, 3, 2):
             to = (x + d) % NX
-            f[k, d] = send(fin.at[k, to], fbuf.at[x, rows], f_s.at[k, d - 1], f_r.at[k, d - 1], dev(dx=d))
-    for k in (2, 0, 3, 1):
-        rows = slice(k * Q, (k + 1) * Q)
-        for d in (0, 1, 3, 2):
-            src = (x + NX - d) % NX
-            if d == 0:
-                value = fin[k, x].astype(F32)
-            else:
-                f[k, d].wait_recv()
-                value = fbuf[src, rows].astype(F32)
-            gate_out[rows, lanes(src)] = (value * gate_f[rows, lanes(src)]).astype(BF16)
-            up_out[rows, lanes(src)] = (value * up_f[rows, lanes(src)]).astype(BF16)
-
-    for copy in sent:
-        copy.wait_send()
+            f[k, d] = send(fin.at[k, to], fbuf.at[i, x], f_s.at[i, d - 1], f_r.at[i, d - 1], dev(dx=d))
+        fbuf[i, x] = fin[k, x]
+
+    def result(k, src, value):
+        rows, cols = slice(k * Q, (k + 1) * Q), slice(src * SUB, (src + 1) * SUB)
+        gate_out[rows, cols] = (value * gate_f[rows, cols]).astype(BF16)
+        up_out[rows, cols] = (value * up_f[rows, cols]).astype(BF16)
+
+    for i, k in enumerate((2, 0)):
+        for d in (1, 3, 2):
+            f[k, d].wait_recv()
+        for src in range(NX):
+            result(k, src, fbuf[i, src].astype(F32))
+    for i, k in enumerate(early):
+        wait_swap(2, k)
+        for way in (R, L):
+            rs[way, 3, k].wait_recv()
+        for src in range(NX):
+            value = x_land[2, i, src].astype(F32)
+            for way in (R, L):
+                value = value + rs_recv[way, 3, k, src].astype(F32)
+            result(k, src, value)
+
+    drain(len(sent))
 
 
 def copy_out(*refs):
@@ -300,21 +368,23 @@
             pltpu.VMEM((2, 4, NQ, NX, Q, SUB), BF16),
             pltpu.VMEM((2, 4, NQ, NX, Q, SUB), BF16),
             pltpu.VMEM((NQ, NX, Q, SUB), BF16),
-            pltpu.VMEM((NX, TOK, SUB), BF16),
+            pltpu.VMEM((2, NX, Q, SUB), BF16),
             pltpu.VMEM((TOK, NX * SUB), F32),
             pltpu.VMEM((TOK, NX * SUB), F32),
             pltpu.VMEM((SUB, DG), F32),
             pltpu.VMEM((NX, SUB, DB), BF16),
             pltpu.VMEM((NX, SUB, DB), BF16),
-            dma((4,)),
+            pltpu.VMEM((3, 2, NX, Q, SUB), BF16),
+            dma((4, 2)), dma((2,)),
             dma((3,)), dma((3,)),
             dma((3,)), dma((3,)),
-            dma((4, 3)), dma((4, 3)),
-            dma((4,)), dma((4,)),
+            dma((4, 4)), dma((4, 4)),
+            dma((4, 5)), dma((4, 5)),
             dma((3,)), dma((3,)),
             dma((2, 4, 4)), dma((2, 4, 4)),
             dma((2, 4, NQ)), dma((2, 4, NQ)),
-            dma((NQ, 3)), dma((NQ, 3)),
+            dma((2, 3)), dma((2, 3)),
+            dma((3, 2, 3)), dma((3, 2, 3)),
             dma((3,)), dma((3,)),
         ],
         compiler_params=pltpu.CompilerParams(

time: 91.9 us -> 87.9 us (0.956)
  the two profiles are of different devices: /device:TPU:64 before, /device:TPU:2 now
where the time goes in v3:
time: 87.9 us; the launch traced here: 87.8 us
  Pallas kernels  87.2 us (99%)
    pallas_call x1, Pallas kernels, shards(): pl.pallas_call(kernel, out_shape=[pltpu.VMEM(*shape) for shape in shapes]...  85 us
    pallas_call x1, Pallas kernels, shards(): pl.pallas_call(copy_out, out_shape=[jax.ShapeDtypeStruct(*shape) for shap...  2.15 us

profile of v3, /device:TPU:2, one launch (start us, length us, event | category | flops | bytes accessed | tf_op | source)
XLA Modules:
  0.0 87.8 jit_solution(1369403453745906958)
XLA Ops:
  0.6 85.0 %shard_map.67 = (f32[3584,256]{1,0:T(8,128)S(1)}, bf16[64,3584]{1,0:T(8,128)(2,1)S(1)}, bf16[64,3584]{1,0:T(8,128)(2,1)S(1)}) custom-call(bf16[4,64,256]{2,1,0:T(8,128)(2,1)} %bitcast.1, bf16[64,3584]{1,0:T(8,128)(2,1)} %gate.1, bf16[64,3584]{1,0:T(8,128)(2,1)} %up.1, bf16[3584,256]{1,0:T(8,128)(2,1)} %w.1), custom_call_target="tpu_custom_call" | custom-call | tf_op jit(solution)/shard_map/pallas_call | solution.py:355
  85.7 2.2 %shard_map.68 = (f32[3584,256]{1,0:T(8,128)}, bf16[64,3584]{1,0:T(8,128)(2,1)}, bf16[64,3584]{1,0:T(8,128)(2,1)}) custom-call(f32[3584,256]{1,0:T(8,128)S(1)} %get-tuple-element.6.refs_0_, bf16[64,3584]{1,0:T(8,128)(2,1)S(1)} %get-tuple-element.7.refs_1_, bf16[64,3584]{1,0:T(8,128)(2,1)S(1)} %get-tuple-element.8.refs_2_), custom_call_target="tpu_custom_call" | custom-call | tf_op jit(solution)/shard_map/pallas_call | solution.py:394

commit v4 on v3

--- a/solution.py
+++ b/solution.py
@@ -14,6 +14,7 @@
 BLK = NX * TOK
 Q = 16
 NQ = TOK // Q
+OWN = 2
 R, L = 0, 1
 F32, BF16 = jnp.float32, jnp.bfloat16
 
@@ -88,15 +89,19 @@
 
     def gather(hop, d):
         src = (x + NX - d) % NX
+        parts = OWN if d == 0 else 1
+        n = TOK // parts
         for way in (R, L):
-            if hop > 1 and hop - 1 <= last_hop(way, d):
-                ag[way, hop - 1, d].wait_recv()
-            if hop <= last_hop(way, d):
-                b = (z - (hop - 1) + NZ) % NZ if way == R else (z + (hop - 1)) % NZ
-                piece = hh.at[b, at(src, TOK)]
-                ag[way, hop, d] = send(
-                    piece, piece, ag_s.at[way, hop - 1, d], ag_r.at[way, hop - 1, d], dev(dz=1 if way == R else -1)
-                )
+            for i in range(parts):
+                j = i if d == 0 else OWN + d - 1
+                if hop > 1 and hop - 1 <= last_hop(way, d):
+                    ag[way, hop - 1, j].wait_recv()
+                if hop <= last_hop(way, d):
+                    b = (z - (hop - 1) + NZ) % NZ if way == R else (z + (hop - 1)) % NZ
+                    piece = hh.at[b, pl.ds(pl.multiple_of(src * TOK + i * n, n), n)]
+                    ag[way, hop, j] = send(
+                        piece, piece, ag_s.at[way, hop - 1, j], ag_r.at[way, hop - 1, j], dev(dz=1 if way == R else -1)
+                    )
 
     gather(1, 0)
 
@@ -135,6 +140,7 @@
 
     load_g.wait()
     spread(0)
+    gather(2, 0)
     for d in (1, 3):
         hid_copies[d].wait_recv()
         gather(1, d)
@@ -147,7 +153,6 @@
     for d in (1, 3, 2):
         to = (x + d) % NX
         w_copies.append(send(w.at[at(to, SUB)], wg.at[:, at(x, DB)], w_s.at[d - 1], w_r.at[d - 1], dev(dx=d)))
-    gather(2, 0)
     relay(0)
     gather(2, 1)
     for d in (1, 3):
@@ -213,8 +218,8 @@
     rs = {}
 
     order = {
-        R: ((1, 0), (3, 2, 1, 0), (3, 1, 2, 0), (2, 0)),
-        L: ((3, 2), (1, 0, 3, 2), (1, 3, 0, 2), (0, 2)),
+        R: ((1, 0), (3, 2, 1, 0), (3, 2, 0, 1), (2, 0)),
+        L: ((2, 3), (1, 0, 2, 3), (1, 2, 0, 3), (2, 0)),
     }
 
     def running(way, step, k):
@@ -237,7 +242,7 @@
                 rs_send[way, step, k] = running(way, step, k)
                 pass_on(way, step, k, rs_send.at[way, step, k])
 
-    early = (3, 1)
+    early, home = (3, 1), (2, 0)
     swapped = {}
 
     def swap(who, k, src):
@@ -262,8 +267,9 @@
     def _(i):
         multiply((z + 6 + i) % NZ)
 
-    for way, d in ((R, 0), (R, 1), (L, 3), (L, 2)):
-        ag[way, 4, d].wait_recv()
+    for way, js in ((R, range(OWN + 1)), (L, (OWN + 2, OWN + 1))):
+        for j in js:
+            ag[way, 4, j].wait_recv()
     last = (z + 4) % NZ
     dw = {}
     for d in (1, 3, 2, 0):
@@ -284,27 +290,23 @@
     reduce_both(2, (0, 1, 2, 3))
     drain(before)
     before = len(sent)
-    for way, k in ((R, 3), (L, 1), (R, 1), (L, 3)):
-        rs_send[way, 3, k] = running(way, 3, k)
-        swap(way, k, rs_send.at[way, 3, k])
+    def swap_running(pairs):
+        for way, k in pairs:
+            rs_send[way, 3, k] = running(way, 3, k)
+            swap(way, k, rs_send.at[way, 3, k])
+
+    swap_running(((R, 3), (L, 1)))
+    reduce_both(3, (0, 1))
+    swap_running(((R, 1), (L, 3)))
     for k in early:
         fin[k] = part[z, :, k * Q : (k + 1) * Q, :].astype(BF16)
         swap(2, k, fin.at[k])
-    reduce_both(3, (0, 1))
-    for k in early:
-        for way in (R, L):
-            wait_swap(way, k)
-            pass_on(way, 3, k, x_land.at[way, early.index(k)])
-    drain(before)
-    for d in (1, 3, 2):
-        dw[d].wait_recv()
-        src = (x + NX - d) % NX
-        dw_out[at(src, SUB)] = land[src].astype(F32)
 
     f = {}
-    for i, k in enumerate((2, 0)):
-        rows = slice(k * Q, (k + 1) * Q)
-        value = part[z, :, rows, :]
+
+    def give_back(k):
+        i = home.index(k)
+        value = part[z, :, k * Q : (k + 1) * Q, :]
         for way in (R, L):
             rs[way, 3, k].wait_recv()
             value = value + rs_recv[way, 3, k].astype(F32)
@@ -314,12 +316,27 @@
             f[k, d] = send(fin.at[k, to], fbuf.at[i, x], f_s.at[i, d - 1], f_r.at[i, d - 1], dev(dx=d))
         fbuf[i, x] = fin[k, x]
 
+    def last_step(pairs):
+        for way, k in pairs:
+            wait_swap(way, k)
+            pass_on(way, 3, k, x_land.at[way, early.index(k)])
+
+    last_step(((R, 3), (L, 1)))
+    give_back(home[0])
+    last_step(((R, 1), (L, 3)))
+    give_back(home[1])
+    drain(before)
+    for d in (1, 3, 2):
+        dw[d].wait_recv()
+        src = (x + NX - d) % NX
+        dw_out[at(src, SUB)] = land[src].astype(F32)
+
     def result(k, src, value):
         rows, cols = slice(k * Q, (k + 1) * Q), slice(src * SUB, (src + 1) * SUB)
         gate_out[rows, cols] = (value * gate_f[rows, cols]).astype(BF16)
         up_out[rows, cols] = (value * up_f[rows, cols]).astype(BF16)
 
-    for i, k in enumerate((2, 0)):
+    for i, k in enumerate(home):
         for d in (1, 3, 2):
             f[k, d].wait_recv()
         for src in range(NX):
@@ -381,7 +398,7 @@
             dma((4, 4)), dma((4, 4)),
             dma((4, 5)), dma((4, 5)),
             dma((3,)), dma((3,)),
-            dma((2, 4, 4)), dma((2, 4, 4)),
+            dma((2, 4, OWN + 3)), dma((2, 4, OWN + 3)),
             dma((2, 4, NQ)), dma((2, 4, NQ)),
             dma((2, 3)), dma((2, 3)),
             dma((3, 2, 3)), dma((3, 2, 3)),

time: 87.9 us -> 86.5 us (0.984)
  Pallas kernels: 87.2 us -> 85.8 us
    pallas_call x1, Pallas kernels: 85 us -> 83.7 us  [shards(): pl.pallas_call(kernel, out_shape=[pltpu.VMEM(*shape) for shape in shapes]...]
where the time goes in v4:
time: 86.5 us; the launch traced here: 86.4 us
  Pallas kernels  85.8 us (99%)
    pallas_call x1, Pallas kernels, shards(): pl.pallas_call(kernel, out_shape=[pltpu.VMEM(*shape) for shape in shapes]...  83.7 us
    pallas_call x1, Pallas kernels, shards(): pl.pallas_call(copy_out, out_shape=[jax.ShapeDtypeStruct(*shape) for shap...  2.15 us

profile of v4, /device:TPU:2, one launch (start us, length us, event | category | flops | bytes accessed | tf_op | source)
XLA Modules:
  0.0 86.4 jit_solution(9054788960087989752)
XLA Ops:
  0.6 83.7 %shard_map.67 = (f32[3584,256]{1,0:T(8,128)S(1)}, bf16[64,3584]{1,0:T(8,128)(2,1)S(1)}, bf16[64,3584]{1,0:T(8,128)(2,1)S(1)}) custom-call(bf16[4,64,256]{2,1,0:T(8,128)(2,1)} %bitcast.1, bf16[64,3584]{1,0:T(8,128)(2,1)} %gate.1, bf16[64,3584]{1,0:T(8,128)(2,1)} %up.1, bf16[3584,256]{1,0:T(8,128)(2,1)} %w.1), custom_call_target="tpu_custom_call" | custom-call | tf_op jit(solution)/shard_map/pallas_call | solution.py:372
  84.3 2.2 %shard_map.68 = (f32[3584,256]{1,0:T(8,128)}, bf16[64,3584]{1,0:T(8,128)(2,1)}, bf16[64,3584]{1,0:T(8,128)(2,1)}) custom-call(f32[3584,256]{1,0:T(8,128)S(1)} %get-tuple-element.6.refs_0_, bf16[64,3584]{1,0:T(8,128)(2,1)S(1)} %get-tuple-element.7.refs_1_, bf16[64,3584]{1,0:T(8,128)(2,1)S(1)} %get-tuple-element.8.refs_2_), custom_call_target="tpu_custom_call" | custom-call | tf_op jit(solution)/shard_map/pallas_call | solution.py:411

commit v5 on v4

--- a/solution.py
+++ b/solution.py
@@ -203,10 +203,6 @@
     gather(4, 3)
     gather(4, 2)
 
-    @pl.loop(0, 2)
-    def _(i):
-        acc[...] += product((z + 3 + 2 * i) % NZ)
-
     load_w.wait()
     for copy in w_copies:
         copy.wait_recv()
@@ -263,9 +259,12 @@
     multiply((z + 5) % NZ)
     reduce_both(1, (0, 1))
 
-    @pl.loop(0, 5)
+    @pl.loop(0, 2)
     def _(i):
-        multiply((z + 6 + i) % NZ)
+        acc[...] += product((z + 3 + 2 * i) % NZ)
+
+    multiply((z + 2) % NZ)
+    multiply((z + 6) % NZ)
 
     for way, js in ((R, range(OWN + 1)), (L, (OWN + 2, OWN + 1))):
         for j in js:
@@ -285,6 +284,11 @@
 
     before = len(sent) - 11
     reduce_both(1, (2, 3))
+
+    @pl.loop(0, 3)
+    def _(i):
+        multiply((z + 7 + i) % NZ)
+
     drain(before)
     before = len(sent)
     reduce_both(2, (0, 1, 2, 3))

time: 86.5 us -> 85.6 us (0.990)
  Pallas kernels: 85.8 us -> 84.7 us
    pallas_call x1, Pallas kernels: 83.7 us -> 82.5 us  [shards(): pl.pallas_call(kernel, out_shape=[pltpu.VMEM(*shape) for shape in shapes]...]
where the time goes in v5:
time: 85.6 us; the launch traced here: 85.3 us
  Pallas kernels  84.7 us (99%)
    pallas_call x1, Pallas kernels, shards(): pl.pallas_call(kernel, out_shape=[pltpu.VMEM(*shape) for shape in shapes]...  82.5 us
    pallas_call x1, Pallas kernels, shards(): pl.pallas_call(copy_out, out_shape=[jax.ShapeDtypeStruct(*shape) for shap...  2.15 us

profile of v5, /device:TPU:2, one launch (start us, length us, event | category | flops | bytes accessed | tf_op | source)
XLA Modules:
  0.0 85.3 jit_solution(3788333760539000354)
XLA Ops:
  0.6 82.5 %shard_map.67 = (f32[3584,256]{1,0:T(8,128)S(1)}, bf16[64,3584]{1,0:T(8,128)(2,1)S(1)}, bf16[64,3584]{1,0:T(8,128)(2,1)S(1)}) custom-call(bf16[4,64,256]{2,1,0:T(8,128)(2,1)} %bitcast.1, bf16[64,3584]{1,0:T(8,128)(2,1)} %gate.1, bf16[64,3584]{1,0:T(8,128)(2,1)} %up.1, bf16[3584,256]{1,0:T(8,128)(2,1)} %w.1), custom_call_target="tpu_custom_call" | custom-call | tf_op jit(solution)/shard_map/pallas_call | solution.py:376
  83.2 2.2 %shard_map.68 = (f32[3584,256]{1,0:T(8,128)}, bf16[64,3584]{1,0:T(8,128)(2,1)}, bf16[64,3584]{1,0:T(8,128)(2,1)}) custom-call(f32[3584,256]{1,0:T(8,128)S(1)} %get-tuple-element.6.refs_0_, bf16[64,3584]{1,0:T(8,128)(2,1)S(1)} %get-tuple-element.7.refs_1_, bf16[64,3584]{1,0:T(8,128)(2,1)S(1)} %get-tuple-element.8.refs_2_), custom_call_target="tpu_custom_call" | custom-call | tf_op jit(solution)/shard_map/pallas_call | solution.py:415

commit v6 on v5

--- a/solution.py
+++ b/solution.py
@@ -263,9 +263,6 @@
     def _(i):
         acc[...] += product((z + 3 + 2 * i) % NZ)
 
-    multiply((z + 2) % NZ)
-    multiply((z + 6) % NZ)
-
     for way, js in ((R, range(OWN + 1)), (L, (OWN + 2, OWN + 1))):
         for j in js:
             ag[way, 4, j].wait_recv()
@@ -283,6 +280,8 @@
             dw[d] = send(dws.at[to], land.at[x], dw_s.at[d - 1], dw_r.at[d - 1], dev(dx=d))
 
     before = len(sent) - 11
+    multiply((z + 2) % NZ)
+    multiply((z + 6) % NZ)
     reduce_both(1, (2, 3))
 
     @pl.loop(0, 3)

time: 85.6 us -> 85.6 us (level)
  no operation moved by 1% of the time
where the time goes in v6:
time: 85.6 us; the launch traced here: 85.3 us
  Pallas kernels  84.7 us (99%)
    pallas_call x1, Pallas kernels, shards(): pl.pallas_call(kernel, out_shape=[pltpu.VMEM(*shape) for shape in shapes]...  82.5 us
    pallas_call x1, Pallas kernels, shards(): pl.pallas_call(copy_out, out_shape=[jax.ShapeDtypeStruct(*shape) for shap...  2.15 us

profile of v6, /device:TPU:2, one launch (start us, length us, event | category | flops | bytes accessed | tf_op | source)
XLA Modules:
  0.0 85.3 jit_solution(6985076868349633598)
XLA Ops:
  0.6 82.5 %shard_map.67 = (f32[3584,256]{1,0:T(8,128)S(1)}, bf16[64,3584]{1,0:T(8,128)(2,1)S(1)}, bf16[64,3584]{1,0:T(8,128)(2,1)S(1)}) custom-call(bf16[4,64,256]{2,1,0:T(8,128)(2,1)} %bitcast.1, bf16[64,3584]{1,0:T(8,128)(2,1)} %gate.1, bf16[64,3584]{1,0:T(8,128)(2,1)} %up.1, bf16[3584,256]{1,0:T(8,128)(2,1)} %w.1), custom_call_target="tpu_custom_call" | custom-call | tf_op jit(solution)/shard_map/pallas_call | solution.py:375
  83.2 2.2 %shard_map.68 = (f32[3584,256]{1,0:T(8,128)}, bf16[64,3584]{1,0:T(8,128)(2,1)}, bf16[64,3584]{1,0:T(8,128)(2,1)}) custom-call(f32[3584,256]{1,0:T(8,128)S(1)} %get-tuple-element.6.refs_0_, bf16[64,3584]{1,0:T(8,128)(2,1)S(1)} %get-tuple-element.7.refs_1_, bf16[64,3584]{1,0:T(8,128)(2,1)S(1)} %get-tuple-element.8.refs_2_), custom_call_target="tpu_custom_call" | custom-call | tf_op jit(solution)/shard_map/pallas_call | solution.py:414
